TPU v7x, 512 devices: a whole 4x8x8 slice. The times are simulated.
512 devices in a mesh: lat: 64 (over z, y), batch: 8 (over x, core).
Axes of the slice: x: 4, y: 8, z: 8, core: 2. Of those that a mesh axis runs over, the one named last changes fastest.
Arguments:
- fields: bfloat16 [8, 192, 384, 384], P('batch', 'lat'), may hold values from -6 to 6
- cotangent: bfloat16 [8, 192, 384, 384], P('batch', 'lat'), may hold values from -6 to 6
- weights: bfloat16 [128, 2, 384, 384], P('lat'), may hold values from -0.21875 to 0.21875
- degree_of: int32 [128], replicated, may hold values from 0 to 127, each once
Outputs:
- grad_fields: bfloat16 [8, 192, 384, 384], P('batch', 'lat')
- grad_weights: bfloat16 [128, 2, 384, 384], P('lat')
Inputs may be any that keep to these rules, and one draw needn't show every extreme that they name: `degree_of`: each degree 0 to 127 is held by exactly one slot.
All inputs are finite; a program needn't handle non-finite values.
Results may differ from a plain program's by a relative error of at most 0.018.
Values may be sent and summed in bfloat16 or wider, within the bound.
No kernel may reach another device: no remote copies, remote signals or barrier semaphores. Data moves between devices by JAX's collectives and lax.ppermute only.
A program may use at most 64 MiB of HBM per device.

v0:
```python
import jax
import jax.numpy as jnp
from jax import lax
from jax.sharding import PartitionSpec as P

LATS = 192
LONS = 384
ORDERS = 128
DEGREES = 128
CHANNELS = 384


def in_one_piece(arrays, axis, dim, along):
    widths = [a.shape[along] for a in arrays]
    both = jnp.concatenate(arrays, axis=along)
    out = lax.all_gather(both, axis, axis=dim, tiled=True)
    return tuple(jnp.split(out, [sum(widths[:k]) for k in range(1, len(widths))], axis=along))


def legendre_table(order_ids, lat_count, degree_count):
    colatitude = jnp.pi * (jnp.arange(lat_count, dtype=jnp.float32) + 0.5) / lat_count
    cosine = jnp.cos(colatitude)[None, :]
    log_sine = jnp.log(jnp.sin(colatitude))[None, :]
    order_col = order_ids[:, None]
    order_real = order_col.astype(jnp.float32)
    steps_up = jnp.arange(1, degree_count + 1, dtype=jnp.float32)[None, :]
    factor = jnp.where(
        steps_up <= order_real, 0.5 * jnp.log((2.0 * steps_up + 1.0) / (2.0 * steps_up)), 0.0
    )
    log_start = 0.5 * jnp.log(1.0 / (4.0 * jnp.pi)) + jnp.sum(factor, axis=1, keepdims=True)
    diagonal = jnp.exp(log_start + order_real * log_sine)
    squared = order_real * order_real

    def advance(carry, degree):
        previous, older = carry
        degree_real = degree.astype(jnp.float32)
        lead = jnp.sqrt(
            jnp.maximum(4.0 * degree_real * degree_real - 1.0, 0.0)
            / jnp.maximum(degree_real * degree_real - squared, 1.0)
        )
        lower = degree_real - 1.0
        back = jnp.sqrt(
            jnp.maximum(lower * lower - squared, 0.0) / jnp.maximum(4.0 * lower * lower - 1.0, 1.0)
        )
        general = lead * (cosine * previous - back * older)
        first = jnp.sqrt(2.0 * order_real + 3.0) * cosine * previous
        value = jnp.where(
            degree == order_col,
            diagonal,
            jnp.where(
                degree == order_col + 1, first, jnp.where(degree > order_col + 1, general, 0.0)
            ),
        )
        return ((value, previous), value)

    zeros = jnp.zeros((order_ids.shape[0], lat_count), jnp.float32)
    final_state, table = lax.scan(
        advance, (zeros, zeros), jnp.arange(degree_count, dtype=jnp.int32)
    )
    return jnp.transpose(table, (1, 0, 2))


def spectral_tables(start, ord_dev, degree_of):
    order_ids = start + jnp.arange(ord_dev, dtype=jnp.int32)
    mine = legendre_table(order_ids, LATS, DEGREES)
    selector = (degree_of[:, None] == jnp.arange(DEGREES, dtype=jnp.int32)[None, :]).astype(
        jnp.float32
    )
    chosen = jnp.einsum("mli,jl->mji", mine, selector, precision=lax.Precision.HIGHEST)
    colatitude = jnp.pi * (jnp.arange(LATS, dtype=jnp.float32) + 0.5) / LATS
    quadrature = 2.0 * jnp.pi * jnp.pi / LATS * jnp.sin(colatitude)
    return ((chosen * quadrature[None, None, :]).astype(jnp.bfloat16), chosen.astype(jnp.bfloat16))


def fourier_tables(lon_count, order_count):
    lon_ids = jnp.arange(lon_count, dtype=jnp.int32)[:, None]
    order_ids = jnp.arange(order_count, dtype=jnp.int32)[None, :]
    phase = 2.0 * jnp.pi * (lon_ids * order_ids % lon_count).astype(jnp.float32) / lon_count
    forward = (
        jnp.stack([jnp.cos(phase), -jnp.sin(phase)], axis=2).reshape(lon_count, 2 * order_count)
        / lon_count
    )
    doubled = jnp.where(order_ids == 0, 1.0, 2.0)
    inverse = jnp.stack([doubled * jnp.cos(phase), -doubled * jnp.sin(phase)], axis=2).reshape(
        lon_count, 2 * order_count
    )
    return (forward.astype(jnp.bfloat16), jnp.transpose(inverse).astype(jnp.bfloat16))


def to_orders(values):
    return lax.all_to_all(values, "lat", split_axis=1, concat_axis=0, tiled=True)


def to_degrees(values):
    return lax.all_to_all(values, "lat", split_axis=0, concat_axis=1, tiled=True)


def back_to_orders(values):
    return lax.all_to_all(values, "lat", split_axis=1, concat_axis=0, tiled=True)


def to_bands(values):
    return lax.all_to_all(values, "lat", split_axis=0, concat_axis=1, tiled=True)


def product(spec, left, right):
    return jnp.einsum(spec, left, right, preferred_element_type=jnp.float32)


def apply_filter(coeffs, weights):
    c_real = coeffs[:, :, 0]
    c_imag = coeffs[:, :, 1]
    w_real = weights[:, 0]
    w_imag = weights[:, 1]
    f_real = product("jmsc,jcd->jmsd", c_real, w_real) - product("jmsc,jcd->jmsd", c_imag, w_imag)
    f_imag = product("jmsc,jcd->jmsd", c_real, w_imag) + product("jmsc,jcd->jmsd", c_imag, w_real)
    return jnp.stack([f_real, f_imag], axis=2).astype(jnp.bfloat16)


def adjoint_filter(grads, weights):
    g_real = grads[:, :, 0]
    g_imag = grads[:, :, 1]
    w_real = weights[:, 0]
    w_imag = weights[:, 1]
    a_real = product("jmsd,jcd->jmsc", g_real, w_real) + product("jmsd,jcd->jmsc", g_imag, w_imag)
    a_imag = product("jmsd,jcd->jmsc", g_imag, w_real) - product("jmsd,jcd->jmsc", g_real, w_imag)
    return jnp.stack([a_real, a_imag], axis=2).astype(jnp.bfloat16)


def filter_grad(coeffs, grads):
    c_real = coeffs[:, :, 0]
    c_imag = coeffs[:, :, 1]
    g_real = grads[:, :, 0]
    g_imag = grads[:, :, 1]
    dw_real = product("jmsc,jmsd->jcd", c_real, g_real) + product("jmsc,jmsd->jcd", c_imag, g_imag)
    dw_imag = product("jmsc,jmsd->jcd", c_real, g_imag) - product("jmsc,jmsd->jcd", c_imag, g_real)
    return jnp.stack([dw_real, dw_imag], axis=1)


def local(fields, cotangent, weights, degree_of):
    samples = fields.shape[0]
    band_rows = fields.shape[1]
    ord_dev = ORDERS // lax.axis_size("lat")
    forward, inverse = fourier_tables(LONS, ORDERS)
    qslot, pslot = spectral_tables(lax.axis_index("lat") * ord_dev, ord_dev, degree_of)
    spectra = product("sikc,kf->ifsc", fields, forward).astype(jnp.bfloat16)
    spectra = spectra.reshape(band_rows, ORDERS, 2, samples, CHANNELS)
    gathered = to_orders(spectra)
    coeffs_local = product("mji,imrsc->jmrsc", qslot, gathered).astype(jnp.bfloat16)
    coeffs = to_degrees(coeffs_local)
    filtered = apply_filter(coeffs, weights)
    returned = back_to_orders(filtered)
    synth_local = product("mji,jmrsc->imrsc", pslot, returned).astype(jnp.bfloat16)
    synth = to_bands(synth_local)
    response = product(
        "ifsc,fk->sikc", synth.reshape(band_rows, 2 * ORDERS, samples, CHANNELS), inverse
    )
    activated, pullback = jax.vjp(jax.nn.gelu, response)
    upstream = pullback(cotangent.astype(jnp.float32))[0].astype(jnp.bfloat16)
    grad_synth = product("sikc,fk->ifsc", upstream, inverse).astype(jnp.bfloat16)
    grad_synth = grad_synth.reshape(band_rows, ORDERS, 2, samples, CHANNELS)
    grad_gathered = to_orders(grad_synth)
    grad_local = product("mji,imrsc->jmrsc", pslot, grad_gathered).astype(jnp.bfloat16)
    grad_filtered = to_degrees(grad_local)
    all_coeffs, all_grads = in_one_piece((coeffs, grad_filtered), "batch", 3, 0)
    weight_total = filter_grad(all_coeffs, all_grads)
    grad_coeffs = adjoint_filter(grad_filtered, weights)
    grad_back = back_to_orders(grad_coeffs)
    grad_local_spec = product("mji,jmrsc->imrsc", qslot, grad_back).astype(jnp.bfloat16)
    grad_bands = to_bands(grad_local_spec)
    delta = product(
        "ifsc,kf->sikc", grad_bands.reshape(band_rows, 2 * ORDERS, samples, CHANNELS), forward
    )
    grad_fields = (cotangent.astype(jnp.float32) + delta).astype(jnp.bfloat16)
    return (grad_fields, weight_total.astype(jnp.bfloat16))


def solution(mesh):
    return jax.shard_map(
        local,
        mesh=mesh,
        in_specs=(
            P("batch", "lat", None, None),
            P("batch", "lat", None, None),
            P("lat", None, None, None),
            P(),
        ),
        out_specs=(P("batch", "lat", None, None), P("lat", None, None, None)),
        check_vma=False,
    )
```

profile of v0, /device:TPU:6, one launch (start us, length us, event | category | flops | bytes accessed | tf_op | source)
XLA Modules:
  0.0 588.7 jit_solution(4414124567485048653)
XLA Ops:
  9.7 1.2 copy.172
  11.0 16.6 %all-to-all-start = ((bf16[3,128,2,1,384]{4,2,0,3,1:T(2,128)(2,1)}), bf16[3,128,2,1,384]{4,2,0,3,1:T(2,128)(2,1)S(1)}, u32[]{:S(2)}, u32[]{:S(2)}) async-start(bf16[3,128,2,1,384]{4,2,0,3,1:T(2,128)(2,1)} %copy.172), calls=%async_computation | async-start | bytes 1179648 | tf_op jit(solution)/shard_map/all_to_all | solution.py:91
  27.9 350.0 %while.21 = (s32[]{:T(128)}, f32[2,192]{1,0:T(2,128)S(1)}, f32[2,192]{1,0:T(2,128)S(1)}, f32[128,2,192]{2,1,0:T(2,128)S(1)}, s32[128]{0:T(128)S(1)}, /*index=5*/...) while((s32[]{:T(128)}, f32[2,192]{1,0:T(2,128)S(1)}, ...), condition=%wide.region_2.3_spmd.clone.clone.clone.clone, body=%wide.region_1.2_spmd.clone.clone.clone.clone.sunk | while | flops 5047 | bytes 17529 | solution.py:57
  379.3 1.3 fusion.38
  380.6 1.4 copy.177
  382.0 29.2 %all_to_all.126 = bf16[128,2,2,1,384]{4,2,1,3,0:T(2,128)(2,1)S(1)} all-to-all(bf16[128,2,2,1,384]{4,2,1,3,0:T(2,128)(2,1)S(1)} %copy.177), channel_id=1, replica_groups=mesh['lat'=64,'batch'=8] {'lat'}, dimensions={0} | all-to-all | bytes 786432 | tf_op jit(solution)/shard_map/all_to_all | solution.py:95
  413.3 20.7 %all_to_all.127 = bf16[2,128,2,1,384]{4,0,3,2,1:T(2,128)(2,1)S(1)} all-to-all(bf16[2,128,2,1,384]{4,0,3,2,1:T(2,128)(2,1)S(1)} %copy.181), channel_id=1, replica_groups=mesh['lat'=64,'batch'=8] {'lat'}, dimensions={1} | all-to-all | bytes 786432 | tf_op jit(solution)/shard_map/all_to_all | solution.py:99
  435.2 1.3 fusion.32
  436.5 1.4 copy.183
  437.9 5.5 all-to-all-start.3
  446.2 16.2 %all-to-all-done.3 = bf16[192,2,2,1,384]{4,2,1,3,0:T(2,128)(2,1)} async-done(((bf16[192,2,2,1,384]{4,2,1,3,0:T(2,128)(2,1)}), bf16[192,2,2,1,384]{4,2,1,3,0:T(2,128)(2,1)}, u32[]{:S(2)}, u32[]{:S(2)}) %all-to-all-start.3) | async-done | bytes 589856 | tf_op jit(solution)/shard_map/all_to_all | solution.py:103
  462.4 1.5 copy.184
  463.9 1.0 reshape.469
  464.9 4.0 fusion.36
  468.9 1.9 reshape.471
  471.2 24.4 %all_to_all.128 = bf16[3,128,2,1,384]{4,2,0,3,1:T(2,128)(2,1)S(1)} all-to-all(bf16[3,128,2,1,384]{4,2,0,3,1:T(2,128)(2,1)S(1)} %copy.186), channel_id=1, replica_groups=mesh['lat'=64,'batch'=8] {'lat'}, dimensions={1} | all-to-all | bytes 1179648 | tf_op jit(solution)/shard_map/all_to_all | solution.py:91
  496.4 1.2 fusion.39
  497.6 1.3 copy.190
  498.9 20.7 %all_to_all.129 = bf16[128,2,2,1,384]{4,2,1,3,0:T(2,128)(2,1)S(1)} all-to-all(bf16[128,2,2,1,384]{4,2,1,3,0:T(2,128)(2,1)S(1)} %copy.190), channel_id=1, replica_groups=mesh['lat'=64,'batch'=8] {'lat'}, dimensions={0} | all-to-all | bytes 786432 | tf_op jit(solution)/shard_map/all_to_all | solution.py:95
  519.7 1.0 copy.191
  520.7 1.1 all_to_all.111
  521.9 1.0 pad_maximum_fusion.1
  524.6 19.7 %all_to_all.130 = bf16[2,128,2,1,384]{4,0,3,2,1:T(2,128)(2,1)S(1)} all-to-all(bf16[2,128,2,1,384]{4,0,3,2,1:T(2,128)(2,1)S(1)} %copy.192), channel_id=1, replica_groups=mesh['lat'=64,'batch'=8] {'lat'}, dimensions={1} | all-to-all | bytes 786432 | tf_op jit(solution)/shard_map/all_to_all | solution.py:99
  545.1 1.4 copy.194
  546.5 4.6 all-to-all-start.7
  551.3 18.0 %all-to-all-done.7 = bf16[192,2,2,1,384]{4,2,1,3,0:T(2,128)(2,1)S(1)} async-done(((bf16[192,2,2,1,384]{4,2,1,3,0:T(2,128)(2,1)}), bf16[192,2,2,1,384]{4,2,1,3,0:T(2,128)(2,1)S(1)}, u32[]{:S(2)}, u32[]{:S(2)}) %all-to-all-start.7) | async-done | bytes 589856 | tf_op jit(solution)/shard_map/all_to_all | solution.py:103
  570.0 2.6 fusion.24
  572.5 3.1 convolution_bitcast_fusion.2
  575.6 2.9 convolution_bitcast_fusion
  578.5 1.0 fusion.34
  579.6 1.0 fusion.35
  580.7 1.1 copy.201
  (967 shorter events, 277.0 us)
Async XLA Ops:
  7.2 1.8 copy-start
  8.3 0.7 copy-start.2
  9.7 368.4 %copy-start.5 = (s32[128]{0:T(128)S(1)}, s32[128]{0:T(128)}, u32[]{:S(2)}) copy-start(s32[128]{0:T(128)} %param.9) | copy-start | bytes 1540
  11.0 367.5 %all-to-all-start = ((bf16[3,128,2,1,384]{4,2,0,3,1:T(2,128)(2,1)}), bf16[3,128,2,1,384]{4,2,0,3,1:T(2,128)(2,1)S(1)}, u32[]{:S(2)}, u32[]{:S(2)}) async-start(bf16[3,128,2,1,384]{4,2,0,3,1:T(2,128)(2,1)} %copy.172), calls=%async_computation | async-start | bytes 1179648 | tf_op jit(solution)/shard_map/all_to_all | solution.py:91
  380.6 31.1 %copy-start.1 = (bf16[2,2,384,384]{3,2,1,0:T(8,128)(2,1)S(1)}, bf16[2,2,384,384]{3,2,1,0:T(8,128)(2,1)}, u32[]{:S(2)}) copy-start(bf16[2,2,384,384]{3,2,1,0:T(8,128)(2,1)} %param.8) | copy-start | bytes 3538948
  437.9 24.5 %all-to-all-start.3 = ((bf16[192,2,2,1,384]{4,2,1,3,0:T(2,128)(2,1)}), bf16[192,2,2,1,384]{4,2,1,3,0:T(2,128)(2,1)}, u32[]{:S(2)}, u32[]{:S(2)}) async-start(bf16[192,2,2,1,384]{4,2,1,3,0:T(2,128)(2,1)} %copy.183), calls=%async_computation.3 | async-start | bytes 1179648 | tf_op jit(solution)/shard_map/all_to_all | solution.py:103
  443.4 129.2 %all-gather.2.cloned.1.call-start = ((), (), s32[]{:S(2)}) async-start(), calls=%async_computation.8 | async-start | bytes 7077888 | tf_op jit(solution)/shard_map/all_gather | solution.py:16
  446.2 18.7 %copy-start.4 = (bf16[384,256]{0,1:T(8,128)(2,1)S(1)}, bf16[384,256]{0,1:T(8,128)(2,1)}, u32[]{:S(2)}) copy-start(bf16[384,256]{0,1:T(8,128)(2,1)} %convert_element_type.174) | copy-start | bytes 589828
  544.7 6.4 %copy-start.3 = (bf16[384,128,2]{0,2,1:T(2,128)(2,1)S(1)}, bf16[384,128,2]{0,2,1:T(2,128)(2,1)}, u32[]{:S(2)}) copy-start(bf16[384,128,2]{0,2,1:T(2,128)(2,1)} %copy-done.2) | copy-start | bytes 589828
  546.5 22.8 %all-to-all-start.7 = ((bf16[192,2,2,1,384]{4,2,1,3,0:T(2,128)(2,1)}), bf16[192,2,2,1,384]{4,2,1,3,0:T(2,128)(2,1)S(1)}, u32[]{:S(2)}, u32[]{:S(2)}) async-start(bf16[192,2,2,1,384]{4,2,1,3,0:T(2,128)(2,1)} %copy.194), calls=%async_computation.7 | async-start | bytes 1179648 | tf_op jit(solution)/shard_map/all_to_all | solution.py:103
  572.5 6.0 %copy-start.6 = (bf16[4,128,2,8,384]{4,1,0,3,2:T(8,128)(2,1)S(1)}, bf16[4,128,2,8,384]{4,1,0,3,2:T(8,128)(2,1)}, u32[]{:S(2)}) copy-start(bf16[4,128,2,8,384]{4,1,0,3,2:T(8,128)(2,1)} %all-gather.2.cloned.1.call-done) | copy-start | bytes 18874372
Sparse Core Ops, SparseCore 0:
  523.0 36.7 all-gather.1
where the time goes:
time: 595 us; the launch traced here: 589 us
  other arithmetic  189 us (32%)
  blocking collectives  115 us (19%)
  local copies, waits for them, and re-layouts  99.9 us (17%)
  loops' own time  87.7 us (15%)
  waiting for transfers between devices  34.3 us (6%)
  starting transfers between devices  26.9 us (5%)
  matrix products  21.9 us (4%)
  between operations  14.5 us (2%)
    another operation x1, loops' own time, legendre_table(): lax.scan(advance, (zeros, zeros), jnp.arange(degree_count, dtype=jnp.int32))  87.7 us
    gt x128, other arithmetic, advance(): degree > order_col + 1  81.7 us
    eq x128, other arithmetic, advance(): degree == order_col  80.8 us
    dynamic_slice x128, local copies, waits for them, and re-layouts, legendre_table(): lax.scan(advance, (zeros, zeros), jnp.arange(degree_count, dtype=jnp.int32))  76.7 us
    all_to_all x2, blocking collectives, to_degrees(): lax.all_to_all(values, 'lat', split_axis=0, concat_axis=1, tiled=True)  50 us
    all_to_all x2, blocking collectives, back_to_orders(): lax.all_to_all(values, 'lat', split_axis=1, concat_axis=0, tiled=True)  40.3 us
    all_to_all x2, waiting for transfers between devices, to_bands(): lax.all_to_all(values, 'lat', split_axis=0, concat_axis=1, tiled=True)  34.3 us
    all_to_all x1, blocking collectives, to_orders(): lax.all_to_all(values, 'lat', split_axis=1, concat_axis=0, tiled=True)  24.4 us
  transfers between devices with their start and end apart: 4, of which 2 were waited for; matrix products, arithmetic and copies ran while one was open for 46% of the time, Pallas kernels for 0%

commit v1 on v0

--- a/solution.py
+++ b/solution.py
@@ -8,6 +8,13 @@
 ORDERS = 128
 DEGREES = 128
 CHANNELS = 384
+
+
+def trade_parts(x, axis, split, join):
+    n_dev = lax.axis_size(axis)
+    tiles = jnp.stack(jnp.split(x, n_dev, axis=split), axis=0)
+    tiles = lax.all_to_all(tiles, axis, split_axis=0, concat_axis=0)
+    return jnp.concatenate(tiles, axis=join)
 
 
 def in_one_piece(arrays, axis, dim, along):
@@ -96,7 +103,7 @@
 
 
 def back_to_orders(values):
-    return lax.all_to_all(values, "lat", split_axis=1, concat_axis=0, tiled=True)
+    return trade_parts(values, "lat", 1, 0)
 
 
 def to_bands(values):

time: 595 us -> 622 us (1.045)
  other arithmetic: 189 us -> 206 us
  loops' own time: 87.7 us -> 96.1 us
  local copies, waits for them, and re-layouts: 99.9 us -> 107 us
    eq x128, other arithmetic: 80.8 us -> 89.2 us  [advance(): degree == order_col]
    another operation x1, loops' own time: 87.7 us -> 96.1 us  [legendre_table(): lax.scan(advance, (zeros, zeros), jnp.arange(degree_count, dtype=jnp.int32))]
    gt x128, other arithmetic: 81.7 us -> 90.1 us  [advance(): degree > order_col + 1]
    dynamic_slice x128, local copies, waits for them, and re-layouts: 76.7 us -> 85 us  [legendre_table(): lax.scan(advance, (zeros, zeros), jnp.arange(degree_count, dtype=jnp.int32))]
  transfers between devices with their start and end apart: 4 -> 4, of which waited for: 2 -> 2; matrix products, arithmetic and copies ran while one was open for 46% -> 48% of each run, Pallas kernels for 0% -> 0%
where the time goes in v1:
time: 622 us; the launch traced here: 616 us
  other arithmetic  206 us (33%)
  blocking collectives  113 us (18%)
  local copies, waits for them, and re-layouts  107 us (17%)
  loops' own time  96.1 us (15%)
  waiting for transfers between devices  32.2 us (5%)
  starting transfers between devices  26.9 us (4%)
  matrix products  20.9 us (3%)
  between operations  15 us (2%)
    another operation x1, loops' own time, legendre_table(): lax.scan(advance, (zeros, zeros), jnp.arange(degree_count, dtype=jnp.int32))  96.1 us
    gt x128, other arithmetic, advance(): degree > order_col + 1  90.1 us
    eq x128, other arithmetic, advance(): degree == order_col  89.2 us
    dynamic_slice x128, local copies, waits for them, and re-layouts, legendre_table(): lax.scan(advance, (zeros, zeros), jnp.arange(degree_count, dtype=jnp.int32))  85 us
    all_to_all x2, blocking collectives, to_degrees(): lax.all_to_all(values, 'lat', split_axis=0, concat_axis=1, tiled=True)  49.2 us
    all_to_all x2, blocking collectives, trade_parts(): tiles = lax.all_to_all(tiles, axis, split_axis=0, concat_axis=0)  39.7 us
    all_to_all x2, waiting for transfers between devices, to_bands(): lax.all_to_all(values, 'lat', split_axis=0, concat_axis=1, tiled=True)  32.2 us
    all_to_all x1, blocking collectives, to_orders(): lax.all_to_all(values, 'lat', split_axis=1, concat_axis=0, tiled=True)  24 us
  transfers between devices with their start and end apart: 4, of which 2 were waited for; matrix products, arithmetic and copies ran while one was open for 48% of the time, Pallas kernels for 0%

profile of v1, /device:TPU:6, one launch (start us, length us, event | category | flops | bytes accessed | tf_op | source)
XLA Modules:
  0.0 616.4 jit_solution(14163232432339468117)
XLA Ops:
  9.1 1.2 copy.930
  10.3 16.6 %all-to-all-start = ((bf16[3,128,2,1,384]{4,2,0,3,1:T(2,128)(2,1)}), bf16[3,128,2,1,384]{4,2,0,3,1:T(2,128)(2,1)S(1)}, u32[]{:S(2)}, u32[]{:S(2)}) async-start(bf16[3,128,2,1,384]{4,2,0,3,1:T(2,128)(2,1)} %copy.930), calls=%async_computation | async-start | bytes 1179648 | tf_op jit(solution)/shard_map/all_to_all | solution.py:98
  27.2 383.5 %while.21 = (s32[]{:T(128)}, f32[2,192]{1,0:T(2,128)S(1)}, f32[2,192]{1,0:T(2,128)S(1)}, f32[128,2,192]{2,1,0:T(2,128)S(1)}, s32[128]{0:T(128)S(1)}, /*index=5*/...) while((s32[]{:T(128)}, f32[2,192]{1,0:T(2,128)S(1)}, ...), condition=%wide.region_2.3_spmd.clone.clone.clone.clone, body=%wide.region_1.2_spmd.clone.clone.clone.clone.sunk | while | flops 5047 | bytes 17529 | solution.py:64
  413.1 29.2 %all_to_all.106 = bf16[128,2,2,1,384]{4,2,1,3,0:T(2,128)(2,1)S(1)} all-to-all(bf16[128,2,2,1,384]{4,2,1,3,0:T(2,128)(2,1)S(1)} %copy.935), channel_id=1, replica_groups=mesh['lat'=64,'batch'=8] {'lat'}, dimensions={0} | all-to-all | bytes 786432 | tf_op jit(solution)/shard_map/all_to_all | solution.py:102
  445.3 20.7 %all_to_all.107 = bf16[64,2,2,2,1,384]{5,2,1,3,4,0:T(2,128)(2,1)S(1)} all-to-all(bf16[64,2,2,2,1,384]{5,2,1,3,4,0:T(2,128)(2,1)S(1)} %constant_dynamic-update-slice_fusion), channel_id=1, replica_groups=mesh['lat'=64,'batch'=8] {'lat'}, dimensions={0} | all-to-all | bytes 786432 | tf_op jit(solution)/shard_map/all_to_all | solution.py:16
  466.6 1.4 copy.1004
  468.0 5.6 all-to-all-start.3
  473.8 0.8 multiply_convert_fusion.1
  476.3 16.1 %all-to-all-done.3 = bf16[192,2,2,1,384]{4,2,1,3,0:T(2,128)(2,1)} async-done(((bf16[192,2,2,1,384]{4,2,1,3,0:T(2,128)(2,1)}), bf16[192,2,2,1,384]{4,2,1,3,0:T(2,128)(2,1)}, u32[]{:S(2)}, u32[]{:S(2)}) %all-to-all-start.3) | async-done | bytes 589856 | tf_op jit(solution)/shard_map/all_to_all | solution.py:110
  492.5 1.5 copy.1005
  494.0 1.0 reshape.471
  495.0 4.1 fusion.36
  499.1 1.9 reshape.473
  501.4 24.0 %all_to_all.108 = bf16[3,128,2,1,384]{4,2,0,3,1:T(2,128)(2,1)S(1)} all-to-all(bf16[3,128,2,1,384]{4,2,0,3,1:T(2,128)(2,1)S(1)} %copy.1007), channel_id=1, replica_groups=mesh['lat'=64,'batch'=8] {'lat'}, dimensions={1} | all-to-all | bytes 1179648 | tf_op jit(solution)/shard_map/all_to_all | solution.py:98
  526.2 1.2 fusion.39
  527.4 1.3 copy.1011
  528.8 19.9 %all_to_all.109 = bf16[128,2,2,1,384]{4,2,1,3,0:T(2,128)(2,1)S(1)} all-to-all(bf16[128,2,2,1,384]{4,2,1,3,0:T(2,128)(2,1)S(1)} %copy.1011), channel_id=1, replica_groups=mesh['lat'=64,'batch'=8] {'lat'}, dimensions={0} | all-to-all | bytes 786432 | tf_op jit(solution)/shard_map/all_to_all | solution.py:102
  548.7 1.0 copy.1012
  549.7 1.1 all_to_all.93
  550.9 1.0 pad_maximum_fusion.1
  551.8 1.1 fusion.62
  553.3 1.3 fusion.45
  556.3 19.0 %all_to_all.110 = bf16[64,2,2,2,1,384]{5,2,1,3,4,0:T(2,128)(2,1)S(1)} all-to-all(bf16[64,2,2,2,1,384]{5,2,1,3,4,0:T(2,128)(2,1)S(1)} %constant_dynamic-update-slice_fusion.64), channel_id=1, replica_groups=mesh['lat'=64,'batch'=8] {'lat'}, dimensions={0} | all-to-all | bytes 786432 | tf_op jit(solution)/shard_map/all_to_all | solution.py:16
  576.0 1.4 copy.1078
  577.4 4.6 all-to-all-start.7
  582.1 16.1 %all-to-all-done.7 = bf16[192,2,2,1,384]{4,2,1,3,0:T(2,128)(2,1)S(1)} async-done(((bf16[192,2,2,1,384]{4,2,1,3,0:T(2,128)(2,1)}), bf16[192,2,2,1,384]{4,2,1,3,0:T(2,128)(2,1)S(1)}, u32[]{:S(2)}, u32[]{:S(2)}) %all-to-all-start.7) | async-done | bytes 589856 | tf_op jit(solution)/shard_map/all_to_all | solution.py:110
  598.9 1.4 fusion.24
  600.3 3.1 convolution_bitcast_fusion.2
  603.3 2.9 convolution_bitcast_fusion
  606.2 1.0 fusion.34
  607.3 1.0 fusion.35
  608.5 1.1 copy.1085
  (1087 shorter events, 301.4 us)
Async XLA Ops:
  7.2 1.2 copy-start
  9.1 401.9 %copy-start.3 = (s32[128]{0:T(128)S(1)}, s32[128]{0:T(128)}, u32[]{:S(2)}) copy-start(s32[128]{0:T(128)} %param.9) | copy-start | bytes 1540
  10.3 401.0 %all-to-all-start = ((bf16[3,128,2,1,384]{4,2,0,3,1:T(2,128)(2,1)}), bf16[3,128,2,1,384]{4,2,0,3,1:T(2,128)(2,1)S(1)}, u32[]{:S(2)}, u32[]{:S(2)}) async-start(bf16[3,128,2,1,384]{4,2,0,3,1:T(2,128)(2,1)} %copy.930), calls=%async_computation | async-start | bytes 1179648 | tf_op jit(solution)/shard_map/all_to_all | solution.py:98
  412.6 30.2 %copy-start.1 = (bf16[2,2,384,384]{3,2,1,0:T(8,128)(2,1)S(1)}, bf16[2,2,384,384]{3,2,1,0:T(8,128)(2,1)}, u32[]{:S(2)}) copy-start(bf16[2,2,384,384]{3,2,1,0:T(8,128)(2,1)} %param.8) | copy-start | bytes 3538948
  468.0 24.4 %all-to-all-start.3 = ((bf16[192,2,2,1,384]{4,2,1,3,0:T(2,128)(2,1)}), bf16[192,2,2,1,384]{4,2,1,3,0:T(2,128)(2,1)}, u32[]{:S(2)}, u32[]{:S(2)}) async-start(bf16[192,2,2,1,384]{4,2,1,3,0:T(2,128)(2,1)} %copy.1004), calls=%async_computation.3 | async-start | bytes 1179648 | tf_op jit(solution)/shard_map/all_to_all | solution.py:110
  473.7 126.6 %all-gather.2.cloned.1.call-start = ((), (), s32[]{:S(2)}) async-start(), calls=%async_computation.8 | async-start | bytes 7077888 | tf_op jit(solution)/shard_map/all_gather | solution.py:23
  577.4 20.8 %all-to-all-start.7 = ((bf16[192,2,2,1,384]{4,2,1,3,0:T(2,128)(2,1)}), bf16[192,2,2,1,384]{4,2,1,3,0:T(2,128)(2,1)S(1)}, u32[]{:S(2)}, u32[]{:S(2)}) async-start(bf16[192,2,2,1,384]{4,2,1,3,0:T(2,128)(2,1)} %copy.1078), calls=%async_computation.7 | async-start | bytes 1179648 | tf_op jit(solution)/shard_map/all_to_all | solution.py:110
  582.1 16.8 %copy-start.2 = (bf16[1,3,384,384]{3,2,1,0:T(8,128)(2,1)S(1)}, bf16[1,3,384,384]{3,2,1,0:T(8,128)(2,1)}, u32[]{:S(2)}) copy-start(bf16[1,3,384,384]{3,2,1,0:T(8,128)(2,1)} %param.7) | copy-start | bytes 2654212
  600.3 6.0 copy-start.4
Sparse Core Ops, SparseCore 0:
  553.4 37.0 all-gather.1
